TPU v7x, 32 devices: a whole 2x2x4 slice. The times are simulated.
32 devices in a mesh: group: 2 (over y), expert: 8 (over z, x), tensor: 2 (over core).
Axes of the slice: x: 2, y: 2, z: 4, core: 2. Of those that a mesh axis runs over, the one named last changes fastest.
Arguments:
- tokens: bfloat16 [2048, 4096], P(('group', 'expert'), 'tensor'), parts along dimension 0, may hold values from -6 to 6
- expert_ids: int32 [2048, 2], P(('group', 'expert')), parts along dimension 0, may hold values from 0 to 7, all different within a row; in each aligned block of 128 rows (0 to 127, 128 to 255, ...) at most 40 rows name the same one
- gate_scores: float32 [2048, 2], P(('group', 'expert')), parts along dimension 0, may hold values from 0.05 to 1
- gate_weight: bfloat16 [8, 4096, 768], P('expert', 'tensor'), may hold values from -0.09375 to 0.09375
- up_weight: bfloat16 [8, 4096, 768], P('expert', 'tensor'), may hold values from -0.09375 to 0.09375
- down_weight: bfloat16 [8, 768, 4096], P('expert', None, 'tensor'), may hold values from -0.21875 to 0.21875
Outputs:
- combined: bfloat16 [2048, 4096], P(('group', 'expert'), 'tensor'), parts along dimension 0
There are 2 independent parts, one for each index of `group`. A program takes and returns all parts, laid end to end along the dimension named above; an argument that names none is the same for every part. Nothing has to cross between parts.
Inputs may be any that keep to these rules, and one draw needn't show every extreme that they name: `expert_ids`: the 2 experts of a token differ. Within each aligned block of 128 rows (the rows of one index of expert), no expert is named by more than 40 rows, a bound that some block reaches.
All inputs are finite; a program needn't handle non-finite values.
Results may differ from a plain program's by a relative error of at most 0.0058.
Values may be sent and summed in bfloat16 or wider, within the bound.
A program may use at most 128 MiB of HBM per device.

v0:
```python
import jax
import jax.numpy as jnp
from jax import lax
from jax.sharding import PartitionSpec as P


def expert_apply(slot_block, gate_local, up_local, down_local):
    feature_width = slot_block.shape[-1]
    flat_rows = slot_block.reshape(-1, feature_width)
    gate_part = jnp.dot(flat_rows, gate_local, preferred_element_type=jnp.float32)
    up_part = jnp.dot(flat_rows, up_local, preferred_element_type=jnp.float32)
    gate_share, up_share = (
        lax.psum_scatter(gate_part, "tensor", scatter_dimension=1, tiled=True),
        lax.psum_scatter(up_part, "tensor", scatter_dimension=1, tiled=True),
    )
    hidden_share = (jax.nn.silu(gate_share) * up_share).astype(jnp.bfloat16)
    hidden = lax.all_gather(hidden_share, "tensor", axis=1, tiled=True)
    result = jnp.dot(hidden, down_local, preferred_element_type=jnp.float32).astype(jnp.bfloat16)
    return result.reshape(slot_block.shape)


def shards(tokens, expert_ids, gate_scores, gate_weight, up_weight, down_weight):
    tok_rows, feature_width = tokens.shape
    choose_count = expert_ids.shape[1]
    peer_count = lax.axis_size("expert")
    experts = peer_count * gate_weight.shape[0]
    capacity = max(2, min(tok_rows, 5 * tok_rows * choose_count // (4 * experts)))
    flat_ids = expert_ids.reshape(-1)
    assigned = flat_ids.shape[0]
    onehot = (flat_ids[:, None] == jnp.arange(experts, dtype=jnp.int32)[None, :]).astype(jnp.int32)
    before = jnp.cumsum(onehot, axis=0) - onehot
    slot_index = jnp.sum(before * onehot, axis=1)
    position = flat_ids * capacity + slot_index
    owner_token = jnp.arange(assigned, dtype=jnp.int32) // choose_count
    source_row = jnp.full((experts * capacity,), tok_rows, jnp.int32).at[position].set(owner_token)
    padded = jnp.concatenate((tokens, jnp.zeros((1, feature_width), tokens.dtype)), axis=0)
    outgoing = jnp.take(padded, source_row, axis=0).reshape(experts, capacity, feature_width)
    gate_local = gate_weight[0]
    up_local = up_weight[0]
    down_local = down_weight[0]
    results = expert_apply(
        lax.all_to_all(outgoing, "expert", split_axis=0, concat_axis=0, tiled=True),
        gate_local,
        up_local,
        down_local,
    )
    returned = lax.all_to_all(results, "expert", split_axis=0, concat_axis=0, tiled=True)
    picked = jnp.take(returned.reshape(experts * capacity, feature_width), position, axis=0)
    picked = picked.reshape(tok_rows, choose_count, feature_width)
    gate_norm = gate_scores / jnp.sum(gate_scores, axis=1, keepdims=True)
    combined = jnp.sum(gate_norm[:, :, None] * picked.astype(jnp.float32), axis=1)
    return combined.astype(jnp.bfloat16)


def solution(mesh):
    in_specs = (
        P(("group", "expert"), "tensor"),
        P(("group", "expert"), None),
        P(("group", "expert"), None),
        P("expert", "tensor", None),
        P("expert", "tensor", None),
        P("expert", None, "tensor"),
    )
    out_specs = P(("group", "expert"), "tensor")
    return jax.shard_map(shards, mesh=mesh, in_specs=in_specs, out_specs=out_specs, check_vma=False)
```

profile of v0, /device:TPU:0, one launch (start us, length us, event | category | flops | bytes accessed | tf_op | source)
XLA Modules:
  0.0 146.4 jit_solution(5531948270777665178)
XLA Ops:
  6.5 0.0 copy-start
  6.5 0.0 reduce-scatter.3.cloned.1.call-start
  6.5 0.9 copy.14
  7.5 0.1 eq.26
  7.6 0.1 reshape.85
  7.8 0.7 broadcast_multiply_fusion
  8.5 0.6 reduce-window.6
  9.0 0.2 slice_reduce_fusion
  9.3 0.1 copy.18
  9.4 0.1 mul.41
  9.5 0.1 fusion.10
  9.6 1.4 scatter_custom_fusion
  11.1 0.1 broadcast_in_dim.34
  11.2 1.9 %concatenate.3 = bf16[129,2048]{1,0:T(8,128)(2,1)} pad(bf16[128,2048]{1,0:T(8,128)(2,1)} %param.6, bf16[]{:T(256)} %constant.59.clone.1), padding=0_1x0_0 | pad | bytes 1052674 | tf_op jit(solution)/shard_map/concatenate | solution.py:36
  13.1 6.1 %gather_fusion = bf16[320,2048]{1,0:T(8,128)(2,1)} fusion(bf16[129,2048]{1,0:T(8,128)(2,1)} %concatenate.3, s32[1024]{0:T(1024)S(1)} %pad_clamp_fusion.1), kind=kCustom, calls=%fused_computation | custom fusion | bytes 2622720 | tf_op jit(solution)/shard_map/jit(_take)/gather | solution.py:37
  19.2 0.0 copy-start.4
  19.2 1.6 %broadcast_select_fusion.1 = bf16[8,40,2048]{2,1,0:T(8,128)(2,1)S(1)} fusion(bf16[8,40,2048]{2,1,0:T(8,128)(2,1)} %bitcast.28, pred[8,40]{1,0:T(8,128)(4,1)S(1)} %broadcast_in_dim.34), kind=kLoop, calls=%fused_computation.12 | loop fusion | flops 655360 | bytes 2621760 | tf_op jit(solution)/shard_map/jit(_take)/select_n | solution.py:37
  20.9 38.4 %all_to_all.10 = bf16[8,40,2048]{2,1,0:T(8,128)(2,1)S(1)} all-to-all(bf16[8,40,2048]{2,1,0:T(8,128)(2,1)S(1)} %broadcast_select_fusion.1), channel_id=1, replica_groups=mesh['group'=2,'expert'=8,'tensor'=2] {'expert'}, dimensions={0} | all-to-all | bytes 2621440 | tf_op jit(solution)/shard_map/all_to_all | solution.py:42
  59.3 0.0 copy-start.1
  59.3 1.1 copy-done.1
  60.4 0.0 copy-done.4
  60.4 2.2 %fusion.4 = f32[320,768]{1,0:T(8,128)} fusion(bf16[320,2048]{1,0:T(8,128)(2,1)S(1)} %bitcast.30, bf16[1,2048,768]{2,1,0:T(8,128)(2,1)S(1)} %copy-done.4), kind=kOutput, calls=%fused_computation.7 | convolution fusion | flops 1006632960 | bytes 5439488 | tf_op jit(solution)/shard_map/dot_general | solution.py:10
  62.5 0.0 reduce-scatter.3.cloned.1.call-update
  62.6 0.0 reduce-scatter.5.cloned.1.call-start
  62.6 4.4 %fusion.2 = f32[320,768]{1,0:T(8,128)} fusion(bf16[320,2048]{1,0:T(8,128)(2,1)} %bitcast.31, bf16[1,2048,768]{2,1,0:T(8,128)(2,1)} %param.10), kind=kOutput, calls=%fused_computation.5 | convolution fusion | flops 1006632960 | bytes 5439488 | tf_op jit(solution)/shard_map/dot_general | solution.py:11
  67.1 0.0 reduce-scatter.5.cloned.1.call-update
  67.1 3.2 %reduce-scatter.3.cloned.1.call-done = f32[320,384]{1,0:T(8,128)} async-done(((f32[320,768]{1,0:T(8,128)}), f32[320,384]{1,0:T(8,128)}) %reduce-scatter.3.cloned.1.call-update) | async-done | bytes 491536 | tf_op jit(solution)/shard_map/reduce_scatter | solution.py:13
  70.2 12.0 %reduce-scatter.5.cloned.1.call-done = f32[320,384]{1,0:T(8,128)} async-done(((f32[320,768]{1,0:T(8,128)}), f32[320,384]{1,0:T(8,128)}) %reduce-scatter.5.cloned.1.call-update) | async-done | bytes 491536 | tf_op jit(solution)/shard_map/reduce_scatter | solution.py:14
  82.3 1.3 multiply_convert_fusion
  83.6 2.2 %all_gather.3 = bf16[320,768]{1,0:T(8,128)(2,1)S(1)} all-gather(bf16[320,384]{1,0:T(8,128)(2,1)S(1)} %multiply_convert_fusion), channel_id=1, replica_groups=mesh['group'=2,'expert'=8,'tensor'=2] {'tensor'}, dimensions={1}, use_global_device_ids=true | all-gather | bytes 737280 | tf_op jit(solution)/shard_map/all_gather | solution.py:17
  85.7 0.0 copy-done
  85.7 2.3 %fusion.6 = bf16[320,2048]{1,0:T(8,128)(2,1)} fusion(bf16[320,768]{1,0:T(8,128)(2,1)S(1)} %all_gather.3, bf16[1,768,2048]{2,1,0:T(8,128)(2,1)S(1)} %copy-done), kind=kOutput, calls=%fused_computation.9 | convolution fusion | flops 1007288320 | bytes 4947968 | tf_op jit(solution)/shard_map/dot_general | solution.py:18
  88.0 0.0 copy-start.2
  88.0 0.0 copy-start.3
  88.0 5.9 %all-to-all-start.1 = ((bf16[8,40,2048]{2,1,0:T(8,128)(2,1)}), bf16[8,40,2048]{2,1,0:T(8,128)(2,1)}, u32[]{:S(2)}, u32[]{:S(2)}) async-start(bf16[8,40,2048]{2,1,0:T(8,128)(2,1)} %bitcast.29), calls=%async_computation.3 | async-start | bytes 2621440 | tf_op jit(solution)/shard_map/all_to_all | solution.py:47
  93.9 0.1 reduce_sum.33
  94.1 0.1 copy.16
  94.1 0.0 copy-done.2
  94.2 0.1 copy.17
  94.3 0.0 copy-done.3
  94.3 0.1 copy.13
  94.5 31.4 %all-to-all-done.1 = bf16[8,40,2048]{2,1,0:T(8,128)(2,1)} async-done(((bf16[8,40,2048]{2,1,0:T(8,128)(2,1)}), bf16[8,40,2048]{2,1,0:T(8,128)(2,1)}, u32[]{:S(2)}, u32[]{:S(2)}) %all-to-all-start.1) | async-done | bytes 1310752 | tf_op jit(solution)/shard_map/all_to_all | solution.py:47
  125.9 4.8 %gather_fusion.1 = bf16[256,2048]{1,0:T(8,128)(2,1)} fusion(bf16[320,2048]{1,0:T(8,128)(2,1)} %bitcast.10, s32[1024]{0:T(1024)S(1)} %pad_clamp_fusion), kind=kCustom, calls=%fused_computation.1 | custom fusion | bytes 2098176 | tf_op jit(solution)/shard_map/jit(_take)/gather | solution.py:48
  130.7 2.5 %gather.15 = bf16[128,2,2048]{2,1,0:T(2,128)(2,1)} reshape(bf16[256,2048]{1,0:T(8,128)(2,1)} %gather_fusion.1) | data formatting | bytes 2097152 | tf_op jit(solution)/shard_map/jit(_take)/gather | solution.py:48
  133.3 6.2 %multiply_reduce_fusion = bf16[128,2048]{1,0:T(8,128)(2,1)} fusion(bf16[128,2,2048]{2,1,0:T(2,128)(2,1)} %gather.15, pred[128,2]{1,0:T(8,128)(4,1)S(1)} %copy.17, f32[128,2]{1,0:T(8,128)S(1)} %copy.13), kind=kLoop, calls=%fused_computation.10 | loop fusion | flops 1835008 | bytes 1574144 | tf_op jit(solution)/shard_map/reduce_sum | solution.py:51
  (12 shorter events, 0.1 us)
Async XLA Ops:
  6.5 79.2 %copy-start = (bf16[1,768,2048]{2,1,0:T(8,128)(2,1)S(1)}, bf16[1,768,2048]{2,1,0:T(8,128)(2,1)}, u32[]{:S(2)}) copy-start(bf16[1,768,2048]{2,1,0:T(8,128)(2,1)} %param.11) | copy-start | bytes 9437188
  6.5 63.7 %reduce-scatter.3.cloned.1.call-start = ((), (), s32[]{:S(2)}) async-start(), calls=%async_computation.4 | async-start | bytes 1474560 | tf_op jit(solution)/shard_map/reduce_scatter | solution.py:13
  19.2 41.2 %copy-start.4 = (bf16[1,2048,768]{2,1,0:T(8,128)(2,1)S(1)}, bf16[1,2048,768]{2,1,0:T(8,128)(2,1)}, u32[]{:S(2)}) copy-start(bf16[1,2048,768]{2,1,0:T(8,128)(2,1)} %param.9) | copy-start | bytes 9437188
  59.3 1.1 copy-start.1
  62.6 19.7 %reduce-scatter.5.cloned.1.call-start = ((), (), s32[]{:S(2)}) async-start(), calls=%async_computation.5 | async-start | bytes 1474560 | tf_op jit(solution)/shard_map/reduce_scatter | solution.py:14
  88.0 6.1 %copy-start.2 = (s32[128,2]{0,1:T(2,128)S(1)}, s32[128,2]{0,1:T(2,128)}, u32[]{:S(2)}) copy-start(s32[128,2]{0,1:T(2,128)} %param.7) | copy-start | bytes 3076
  88.0 6.3 %copy-start.3 = (f32[128,2]{0,1:T(2,128)S(1)}, f32[128,2]{0,1:T(2,128)}, u32[]{:S(2)}) copy-start(f32[128,2]{0,1:T(2,128)} %param.8) | copy-start | bytes 3076
  88.0 37.9 %all-to-all-start.1 = ((bf16[8,40,2048]{2,1,0:T(8,128)(2,1)}), bf16[8,40,2048]{2,1,0:T(8,128)(2,1)}, u32[]{:S(2)}, u32[]{:S(2)}) async-start(bf16[8,40,2048]{2,1,0:T(8,128)(2,1)} %bitcast.29), calls=%async_computation.3 | async-start | bytes 2621440 | tf_op jit(solution)/shard_map/all_to_all | solution.py:47
Sparse Core Ops, SparseCore 0:
  62.7 7.5 reduce-scatter.2
  72.6 9.6 reduce-scatter.4
where the time goes:
time: 147 us; the launch traced here: 146 us
  waiting for transfers between devices  46.7 us (32%)
  blocking collectives  40.6 us (28%)
  local copies, waits for them, and re-layouts  20.1 us (14%)
  between operations  13.5 us (9%)
  other arithmetic  10.7 us (7%)
  matrix products  8.89 us (6%)
  starting transfers between devices  5.92 us (4%)
    all_to_all x1, blocking collectives, shards(): lax.all_to_all(outgoing, 'expert', split_axis=0, concat_axis=0, tiled=True)  38.4 us
    all_to_all x1, waiting for transfers between devices, shards(): lax.all_to_all(results, 'expert', split_axis=0, concat_axis=0, tiled=True)  31.4 us
    reduce_scatter x1, waiting for transfers between devices, expert_apply(): lax.psum_scatter(up_part, 'tensor', scatter_dimension=1, tiled=True)  12 us
    gather x2, local copies, waits for them, and re-layouts, shards(): jnp.take(returned.reshape(experts * capacity, feature_width), position, a...  7.38 us
    reduce_sum x1, other arithmetic, shards(): jnp.sum(gate_norm[:, :, None] * picked.astype(jnp.float32), axis=1)  6.24 us
    gather x1, local copies, waits for them, and re-layouts, shards(): jnp.take(padded, source_row, axis=0)  6.1 us
    all_to_all x1, starting transfers between devices, shards(): lax.all_to_all(results, 'expert', split_axis=0, concat_axis=0, tiled=True)  5.88 us
    dot_general x1, matrix products, expert_apply(): up_part = jnp.dot(flat_rows, up_local, preferred_element_type=jnp.float32)  4.44 us
  transfers between devices with their start and end apart: 3, of which 3 were waited for; matrix products, arithmetic and copies ran while one was open for 3% of the time, Pallas kernels for 0%

commit v1 on v0

v1 whole, which is shorter than its diff:
```python
import functools

import jax
import jax.numpy as jnp
from jax import lax
from jax.experimental import pallas as pl
from jax.experimental.pallas import tpu as pltpu
from jax.sharding import PartitionSpec as P

MESH = pl.DeviceIdType.MESH
BF16 = jnp.bfloat16
F32 = jnp.float32
TILE = 512


def column_tile(width):
    return TILE if width % TILE == 0 else width


def layer_kernel(n, ring, ids_ref, gates_ref, tok_ref, wg_hbm, wu_hbm, wd_hbm, out_ref,
                 slot_map, gate_map, outgoing, work, back, part, partner_part, wgu, wd, total,
                 w_sem, go_send, go_recv, part_send, part_recv, ret_send, ret_recv):
    me = lax.axis_index("expert")
    other = 1 - lax.axis_index("tensor")
    rows, width = tok_ref.shape
    slots = work.shape[1]
    hid = wd.shape[0]

    def peer_of(j):
        peer, bit = me, 1
        while bit < n:
            peer = peer + bit * ((j // bit) % 2) * (1 - 2 * ((me // bit) % 2))
            bit *= 2
        return peer

    weights = (
        pltpu.make_async_copy(wg_hbm.at[0], wgu.at[:, pl.ds(0, hid)], w_sem.at[0]),
        pltpu.make_async_copy(wu_hbm.at[0], wgu.at[:, pl.ds(hid, hid)], w_sem.at[1]),
        pltpu.make_async_copy(wd_hbm.at[0], wd, w_sem.at[2]),
    )
    for copy in weights:
        copy.start()

    barrier = pltpu.get_barrier_semaphore()

    def greet(j, carry):
        pl.semaphore_signal(barrier, inc=1, device_id={"expert": peer_of(j)}, device_id_type=MESH)
        return carry

    lax.fori_loop(1, n, greet, 0)
    pl.semaphore_signal(barrier, inc=1, device_id={"tensor": other}, device_id_type=MESH)

    ids = ids_ref[...]
    scores = gates_ref[...]
    norm = scores / jnp.sum(scores, axis=0, keepdims=True)
    expert = lax.broadcasted_iota(jnp.int32, (n, rows), 0)
    mask = jnp.zeros((n, rows), F32)
    gate = jnp.zeros((n, rows), F32)
    for k in range(ids.shape[0]):
        hit = ids[k:k + 1, :] == expert
        mask = mask + jnp.where(hit, 1.0, 0.0)
        gate = gate + jnp.where(hit, norm[k:k + 1, :], 0.0)
    earlier = (lax.broadcasted_iota(jnp.int32, (rows, rows), 0)
               < lax.broadcasted_iota(jnp.int32, (rows, rows), 1))
    before = jnp.dot(mask.astype(BF16), jnp.where(earlier, 1.0, 0.0).astype(BF16),
                     preferred_element_type=F32)
    slot_map[...] = jnp.where(mask > 0.5, before, -1.0)
    gate_map[...] = gate

    def chosen(peer):
        place = lax.broadcasted_iota(jnp.int32, (slots, rows), 0).astype(F32)
        return slot_map[pl.ds(peer, 1), :] == place

    def gathered(peer):
        pick = jnp.where(chosen(peer), 1.0, 0.0).astype(BF16)
        return jnp.dot(pick, tok_ref[...], preferred_element_type=F32).astype(BF16)

    def go(j):
        return pltpu.make_async_remote_copy(
            src_ref=outgoing.at[j], dst_ref=work.at[j], send_sem=go_send.at[j], recv_sem=go_recv.at[j],
            device_id={"expert": peer_of(j)}, device_id_type=MESH)

    def ret(j):
        return pltpu.make_async_remote_copy(
            src_ref=work.at[j], dst_ref=back.at[j], send_sem=ret_send.at[j], recv_sem=ret_recv.at[j],
            device_id={"expert": peer_of(j)}, device_id_type=MESH)

    def swap(j):
        r = j % ring
        return pltpu.make_async_remote_copy(
            src_ref=part.at[r], dst_ref=partner_part.at[r], send_sem=part_send.at[r], recv_sem=part_recv.at[r],
            device_id={"tensor": other}, device_id_type=MESH)

    half = n // 2

    def dispatch(j):
        outgoing[j] = gathered(peer_of(j))
        go(j).start()

    outgoing[half] = gathered(peer_of(half))
    pl.semaphore_wait(barrier, n)
    go(half).start()

    def send_pair(j, carry):
        dispatch(j)
        dispatch(half + j)
        return carry

    lax.fori_loop(1, half, send_pair, 0)
    work[0] = gathered(me)

    up_tile = column_tile(2 * hid)
    down_tile = column_tile(width)

    def project(j):
        r = j % ring

        def tile(c, carry):
            cols = pl.ds(pl.multiple_of(c * up_tile, up_tile), up_tile)
            part[r, :, cols] = jnp.dot(work[j], wgu[:, cols], preferred_element_type=F32)
            return carry

        lax.fori_loop(0, 2 * hid // up_tile, tile, 0)
        swap(j).start()

    def finish(j):
        r = j % ring
        swap(j).wait()
        both = part[r] + partner_part[r]
        pre_gate, pre_up = both[:, :hid], both[:, hid:]
        hidden = (pre_gate / (1.0 + jnp.exp(-pre_gate)) * pre_up).astype(BF16)

        for c in range(width // down_tile):
            cols = pl.ds(c * down_tile, down_tile)
            work[j, :, cols] = jnp.dot(hidden, wd[:, cols], preferred_element_type=F32).astype(BF16)

    def step(i, carry):
        @pl.when(i < n)
        def _():
            @pl.when(i == 0)
            def _():
                weights[0].wait()
                weights[1].wait()

            @pl.when(i > 0)
            def _():
                go(i).wait_recv()

            project(i)

        @pl.when(i > 0)
        def _():
            @pl.when(i == 1)
            def _():
                weights[2].wait()

            finish(i - 1)

            @pl.when(i > 1)
            def _():
                ret(i - 1).start()

        return carry

    lax.fori_loop(0, n + 1, step, 0)

    def weighted(j, block):
        peer = peer_of(j)
        share = jnp.where(chosen(peer), gate_map[pl.ds(peer, 1), :], 0.0)
        high = share.astype(BF16)
        low = (share - high.astype(F32)).astype(BF16)
        sides = jnp.concatenate((high, low), axis=1)
        both = lax.dot_general(sides, block, (((0,), (0,)), ((), ())), preferred_element_type=F32)
        return both[:rows] + both[rows:]

    total[...] = weighted(0, work[0])

    def combine(j, carry):
        ret(j).wait_recv()
        total[...] += weighted(j, back[j])
        return carry

    lax.fori_loop(1, n, combine, 0)
    out_ref[...] = total[...].astype(BF16)

    def drain(j, carry):
        go(j).wait_send()
        ret(j).wait_send()
        return carry

    lax.fori_loop(1, n, drain, 0)


def shards(tokens, expert_ids, gate_scores, gate_weight, up_weight, down_weight):
    rows, width = tokens.shape
    top = expert_ids.shape[1]
    n = lax.axis_size("expert")
    hid = gate_weight.shape[2]
    capacity = max(2, min(rows, 5 * rows * top // (4 * n)))
    slots = -(-capacity // 8) * 8
    ring = min(n, 8)
    vmem = pl.BlockSpec(memory_space=pltpu.VMEM)
    hbm = pl.BlockSpec(memory_space=pl.ANY)
    dma = pltpu.SemaphoreType.DMA
    return pl.pallas_call(
        functools.partial(layer_kernel, n, ring),
        out_shape=jax.ShapeDtypeStruct((rows, width), BF16),
        in_specs=[vmem, vmem, vmem, hbm, hbm, hbm],
        out_specs=vmem,
        scratch_shapes=[
            pltpu.VMEM((n, rows), F32),
            pltpu.VMEM((n, rows), F32),
            pltpu.VMEM((n, slots, width), BF16),
            pltpu.VMEM((n, slots, width), BF16),
            pltpu.VMEM((n, slots, width), BF16),
            pltpu.VMEM((ring, slots, 2 * hid), F32),
            pltpu.VMEM((ring, slots, 2 * hid), F32),
            pltpu.VMEM((width, 2 * hid), BF16),
            pltpu.VMEM((hid, width), BF16),
            pltpu.VMEM((rows, width), F32),
            dma((3,)),
            dma((n,)),
            dma((n,)),
            dma((ring,)),
            dma((ring,)),
            dma((n,)),
            dma((n,)),
        ],
        compiler_params=pltpu.CompilerParams(
            collective_id=0, has_side_effects=True, vmem_limit_bytes=58 * 1024 * 1024),
    )(expert_ids.T, gate_scores.T, tokens, gate_weight, up_weight, down_weight)


def solution(mesh):
    in_specs = (
        P(("group", "expert"), "tensor"),
        P(("group", "expert"), None),
        P(("group", "expert"), None),
        P("expert", "tensor", None),
        P("expert", "tensor", None),
        P("expert", None, "tensor"),
    )
    out_specs = P(("group", "expert"), "tensor")
    return jax.shard_map(shards, mesh=mesh, in_specs=in_specs, out_specs=out_specs, check_vma=False)
```

time: 147 us -> 66.3 us (0.45)
  the two profiles are of different devices: /device:TPU:0 before, /device:TPU:16 now
where the time goes in v1:
time: 66.3 us; the launch traced here: 66.2 us
  Pallas kernels  64.3 us (97%)
  local copies, waits for them, and re-layouts  1.88 us (3%)
    pallas_call x1, Pallas kernels, shards(): pl.pallas_call(functools.partial(layer_kernel, n, ring), out_shape=jax.Sh...  64.3 us
    unnamed x1, local copies, waits for them, and re-layouts  1.88 us

profile of v1, /device:TPU:16, one launch (start us, length us, event | category | flops | bytes accessed | tf_op | source)
XLA Modules:
  0.0 66.2 jit_solution(16763807642592905415)
XLA Ops:
  0.0 64.3 %shard_map.64 = bf16[128,2048]{1,0:T(8,128)(2,1)} custom-call(s32[2,128]{1,0:T(2,128)} %bitcast.2, f32[2,128]{1,0:T(2,128)} %bitcast.3, bf16[128,2048]{1,0:T(8,128)(2,1)} %tok_ref.1, bf16[1,2048,768]{2,1,0:T(8,128)(2,1)} %wg_hbm.1, bf16[1,2048,768]{2,1,0:T(8,128)(2,1)} %wu_hbm.1, bf16[1,768,2048]{2,1,0:T(8,128)(2,1)} %wd_hbm.1), custom_call_target="tpu_custom_call" | custom-call | tf_op jit(solution)/shard_map/pallas_call | solution.py:205
  64.3 1.9 %copy.8 = bf16[128,2048]{1,0:T(8,128)(2,1)} copy(bf16[128,2048]{1,0:T(8,128)(2,1)} %shard_map.64) | data formatting | bytes 1048576

commit v2 on v0

v2 whole, which is shorter than its diff:
```python
import functools

import jax
import jax.numpy as jnp
from jax import lax
from jax.experimental import pallas as pl
from jax.experimental.pallas import tpu as pltpu
from jax.sharding import PartitionSpec as P

MESH = pl.DeviceIdType.MESH
BF16 = jnp.bfloat16
F32 = jnp.float32
TILE = 512


def column_tile(width):
    return TILE if width % TILE == 0 else width


def layer_kernel(n, chunks, ring, ids_ref, gates_ref, tok_ref, wg_hbm, wu_hbm, wd_hbm, out_ref,
                 own_map, far_out_map, far_map, far_tok, outgoing, work, back, part, partner_part,
                 flat, wgu, wd, total, sum_out, sum_in,
                 w_sem, map_sem, far_send, far_recv, go_send, go_recv, part_send, part_recv,
                 ret_send, ret_recv, sum_send, sum_recv, free_sem):
    me = lax.axis_index("expert")
    other = 1 - lax.axis_index("tensor")
    rows, width = tok_ref.shape
    near, slots = work.shape[1], work.shape[2]
    hid = wd.shape[0]
    deep = near * slots
    span = rows // chunks
    sets = 1 + chunks
    far = near + me - 2 * near * (me // near)

    def peer_of(q):
        peer, bit = me, 1
        while bit < near:
            peer = peer + bit * ((q // bit) % 2) * (1 - 2 * ((me // bit) % 2))
            bit *= 2
        return peer

    def send(src, dst, send_sem, recv_sem, to):
        return pltpu.make_async_remote_copy(
            src_ref=src, dst_ref=dst, send_sem=send_sem, recv_sem=recv_sem,
            device_id=to, device_id_type=MESH)

    def go(s, q):
        return send(outgoing.at[s, q], work.at[s, q], go_send.at[s, q], go_recv.at[s, q], {"expert": peer_of(q)})

    def ret(s, q):
        return send(work.at[s, q], back.at[s, q], ret_send.at[s, q], ret_recv.at[s, q], {"expert": peer_of(q)})

    def swap(s):
        r = s % ring
        return send(part.at[r], partner_part.at[r], part_send.at[r], part_recv.at[r], {"tensor": other})

    def cross(r):
        return send(tok_ref.at[pl.ds(r * span, span)], far_tok.at[r], far_send.at[r], far_recv.at[r], {"expert": far})

    def cross_back(r):
        return send(sum_out.at[r], sum_in.at[r], sum_send.at[r], sum_recv.at[r], {"expert": far})

    maps = send(far_out_map, far_map, map_sem.at[0], map_sem.at[1], {"expert": far})

    weights = (
        pltpu.make_async_copy(wg_hbm.at[0], wgu.at[:, pl.ds(0, hid)], w_sem.at[0]),
        pltpu.make_async_copy(wu_hbm.at[0], wgu.at[:, pl.ds(hid, hid)], w_sem.at[1]),
        pltpu.make_async_copy(wd_hbm.at[0], wd, w_sem.at[2]),
    )
    barrier = pltpu.get_barrier_semaphore()
    pl.semaphore_signal(barrier, inc=1, device_id={"expert": far}, device_id_type=MESH)

    def greet(q, carry):
        pl.semaphore_signal(barrier, inc=1, device_id={"expert": peer_of(q)}, device_id_type=MESH)
        return carry

    lax.fori_loop(1, near, greet, 0)
    pl.semaphore_signal(barrier, inc=1, device_id={"tensor": other}, device_id_type=MESH)
    for copy in weights:
        copy.start()
    pl.semaphore_wait(barrier, near + 1)
    cross(0).start()

    ids = ids_ref[...]
    scores = gates_ref[...]
    norm = scores / jnp.sum(scores, axis=0, keepdims=True)
    expert = lax.broadcasted_iota(jnp.int32, (n, rows), 0)
    mask = jnp.zeros((n, rows), F32)
    gate = jnp.zeros((n, rows), F32)
    for k in range(ids.shape[0]):
        hit = ids[k:k + 1, :] == expert
        mask = mask + jnp.where(hit, 1.0, 0.0)
        gate = gate + jnp.where(hit, norm[k:k + 1, :], 0.0)
    first = lax.broadcasted_iota(jnp.int32, (rows, rows), 0)
    second = lax.broadcasted_iota(jnp.int32, (rows, rows), 1)
    earlier = jnp.where(first < second, 1.0, 0.0)

    def slot_of(ahead):
        before = jnp.dot(mask.astype(BF16), ahead.astype(BF16), preferred_element_type=F32)
        return jnp.where(mask > 0.5, before, -1.0)

    own_map[0:n, :] = slot_of(earlier)
    own_map[n:2 * n, :] = gate
    for r in range(1, chunks):
        earlier = jnp.where((first < r * span) & (second >= r * span), 0.0, earlier)
    far_out_map[0:n, :] = slot_of(earlier)
    far_out_map[n:2 * n, :] = gate
    maps.start()

    def row_of(table, index, lo, count):
        line = table[pl.ds(index, 1), :]
        return line if count == rows else line[:, lo:lo + count]

    def chosen(table, peer, lo, count):
        place = lax.broadcasted_iota(jnp.int32, (slots, count), 0).astype(F32)
        return row_of(table, peer, lo, count) == place

    def scatter_out(s, table, lo, count, source):
        pick = jnp.concatenate(
            [jnp.where(chosen(table, peer_of(q), lo, count), 1.0, 0.0) for q in range(near)], axis=0).astype(BF16)
        for c in range(width // column_tile(width)):
            cols = slice(c * column_tile(width), (c + 1) * column_tile(width))
            moved = jnp.dot(pick, source[:, cols], preferred_element_type=F32)
            moved = moved.reshape(near, slots, column_tile(width)).astype(BF16)
            work[s, 0, :, cols] = moved[0]
            for q in range(1, near):
                outgoing[s, q, :, cols] = moved[q]

        def start(q, carry):
            go(s, q).start()
            return carry

        lax.fori_loop(1, near, start, 0)

    def flatten(source, s):
        for c in range(width // column_tile(width)):
            cols = slice(c * column_tile(width), (c + 1) * column_tile(width))
            flat[:, cols] = source[s, :, :, cols].astype(F32).reshape(deep, column_tile(width)).astype(BF16)

    def project(s):
        def arrive(q, carry):
            go(s, q).wait_recv()
            return carry

        lax.fori_loop(1, near, arrive, 0)
        flatten(work, s)
        r = s % ring
        if ring < sets and s > 0:
            pl.semaphore_wait(free_sem, 1)
        up_tile = column_tile(2 * hid)

        def tile(c, carry):
            cols = pl.ds(pl.multiple_of(c * up_tile, up_tile), up_tile)
            part[r, :, cols] = jnp.dot(flat[...], wgu[:, cols], preferred_element_type=F32)
            return carry

        lax.fori_loop(0, 2 * hid // up_tile, tile, 0)
        swap(s).start()

    def finish(s):
        r = s % ring
        swap(s).wait()
        pre_gate = part[r, :, :hid] + partner_part[r, :, :hid]
        pre_up = part[r, :, hid:] + partner_part[r, :, hid:]
        hidden = (pre_gate / (1.0 + jnp.exp(-pre_gate)) * pre_up).astype(BF16)
        if ring < sets and s < sets - 1:
            pl.semaphore_signal(free_sem, inc=1, device_id={"tensor": other}, device_id_type=MESH)
        for c in range(width // column_tile(width)):
            cols = slice(c * column_tile(width), (c + 1) * column_tile(width))
            result = jnp.dot(hidden, wd[:, cols], preferred_element_type=F32)
            result = result.reshape(near, slots, column_tile(width)).astype(BF16)
            back[s, 0, :, cols] = result[0]
            for q in range(1, near):
                work[s, q, :, cols] = result[q]

        def start(q, carry):
            ret(s, q).start()
            return carry

        lax.fori_loop(1, near, start, 0)

    def weighted(s, table, lo, count):
        shares = jnp.concatenate(
            [jnp.where(chosen(table, peer_of(q), lo, count), row_of(table, n + peer_of(q), lo, count), 0.0)
             for q in range(near)], axis=0)
        high = shares.astype(BF16)
        low = (shares - high.astype(F32)).astype(BF16)
        sides = jnp.concatenate((high, low), axis=1)

        def arrive(q, carry):
            ret(s, q).wait_recv()
            return carry

        lax.fori_loop(1, near, arrive, 0)
        flatten(back, s)
        both = lax.dot_general(sides, flat[...], (((0,), (0,)), ((), ())), preferred_element_type=F32)
        return both[:count] + both[count:]

    def relay(r):
        cross(r).wait_recv()
        scatter_out(1 + r, far_map, r * span, span, far_tok.at[r])

    def answer(r):
        sum_out[r] = weighted(1 + r, far_map, r * span, span).astype(BF16)
        cross_back(r).start()

    scatter_out(0, own_map, 0, rows, tok_ref)
    weights[0].wait()
    weights[1].wait()
    project(0)
    for r in range(1, chunks):
        cross(r).start()
    weights[2].wait()
    finish(0)
    maps.wait()
    relay(0)
    project(1)
    finish(1)
    for r in range(1, chunks):
        relay(r)
        answer(r - 1)
        project(1 + r)
        finish(1 + r)
    total[...] = weighted(0, own_map, 0, rows)
    answer(chunks - 1)
    for r in range(chunks):
        cross_back(r).wait_recv()
        lines = slice(r * span, (r + 1) * span)
        out_ref[lines, :] = (total[lines, :] + sum_in[r].astype(F32)).astype(BF16)

    for r in range(chunks):
        cross(r).wait_send()
        cross_back(r).wait_send()
    for s in range(sets):
        def drain(q, carry):
            go(s, q).wait_send()
            ret(s, q).wait_send()
            return carry

        lax.fori_loop(1, near, drain, 0)


def shards(tokens, expert_ids, gate_scores, gate_weight, up_weight, down_weight):
    rows, width = tokens.shape
    top = expert_ids.shape[1]
    n = lax.axis_size("expert")
    hid = gate_weight.shape[2]
    capacity = max(2, min(rows, 5 * rows * top // (4 * n)))
    slots = -(-capacity // 8) * 8
    near = n // 2
    chunks = 2 if n <= 8 else 1
    sets = 1 + chunks
    ring = sets if n <= 8 else 1
    span = rows // chunks
    vmem = pl.BlockSpec(memory_space=pltpu.VMEM)
    hbm = pl.BlockSpec(memory_space=pl.ANY)
    dma = pltpu.SemaphoreType.DMA
    return pl.pallas_call(
        functools.partial(layer_kernel, n, chunks, ring),
        out_shape=jax.ShapeDtypeStruct((rows, width), BF16),
        in_specs=[vmem, vmem, vmem, hbm, hbm, hbm],
        out_specs=vmem,
        scratch_shapes=[
            pltpu.VMEM((2 * n, rows), F32),
            pltpu.VMEM((2 * n, rows), F32),
            pltpu.VMEM((2 * n, rows), F32),
            pltpu.VMEM((chunks, span, width), BF16),
            pltpu.VMEM((sets, near, slots, width), BF16),
            pltpu.VMEM((sets, near, slots, width), BF16),
            pltpu.VMEM((sets, near, slots, width), BF16),
            pltpu.VMEM((ring, near * slots, 2 * hid), F32),
            pltpu.VMEM((ring, near * slots, 2 * hid), F32),
            pltpu.VMEM((near * slots, width), BF16),
            pltpu.VMEM((width, 2 * hid), BF16),
            pltpu.VMEM((hid, width), BF16),
            pltpu.VMEM((rows, width), F32),
            pltpu.VMEM((chunks, span, width), BF16),
            pltpu.VMEM((chunks, span, width), BF16),
            dma((3,)),
            dma((2,)),
            dma((chunks,)),
            dma((chunks,)),
            dma((sets, near)),
            dma((sets, near)),
            dma((ring,)),
            dma((ring,)),
            dma((sets, near)),
            dma((sets, near)),
            dma((chunks,)),
            dma((chunks,)),
            pltpu.SemaphoreType.REGULAR,
        ],
        compiler_params=pltpu.CompilerParams(
            collective_id=0, has_side_effects=True, vmem_limit_bytes=60 * 1024 * 1024),
    )(expert_ids.T, gate_scores.T, tokens, gate_weight, up_weight, down_weight)


def solution(mesh):
    in_specs = (
        P(("group", "expert"), "tensor"),
        P(("group", "expert"), None),
        P(("group", "expert"), None),
        P("expert", "tensor", None),
        P("expert", "tensor", None),
        P("expert", None, "tensor"),
    )
    out_specs = P(("group", "expert"), "tensor")
    return jax.shard_map(shards, mesh=mesh, in_specs=in_specs, out_specs=out_specs, check_vma=False)
```

time: 147 us -> 101 us (0.69)
  Pallas kernels: 0 us -> 99.1 us
  waiting for transfers between devices: 46.7 us -> 0 us
  blocking collectives: 40.6 us -> 0 us
  local copies, waits for them, and re-layouts: 20.1 us -> 1.88 us
  between operations: 13.5 us -> 0.01 us
  other arithmetic: 10.7 us -> 0 us
  matrix products: 8.89 us -> 0 us
  starting transfers between devices: 5.92 us -> 0 us
    pallas_call x0 -> x1, Pallas kernels: none -> 99.1 us  [shards(): pl.pallas_call(functools.partial(layer_kernel, n, chunks, ring), out_shap...]
    all_to_all x1 -> x0, blocking collectives: 38.4 us -> none  [shards(): lax.all_to_all(outgoing, 'expert', split_axis=0, concat_axis=0, tiled=True)]
    all_to_all x1 -> x0, waiting for transfers between devices: 31.4 us -> none  [shards(): lax.all_to_all(results, 'expert', split_axis=0, concat_axis=0, tiled=True)]
    reduce_scatter x2 -> x0, waiting for transfers between devices: 15.2 us -> none  [the longest x1 12 us: expert_apply(): lax.psum_scatter(up_part, 'tensor', scatter_dimension=1, tiled=True)]
    gather x3 -> x0, local copies, waits for them, and re-layouts: 13.5 us -> none  [the longest x2 7.38 us: shards(): jnp.take(returned.reshape(experts * capacity, feature_width), position, a...]
    dot_general x3 -> x0, matrix products: 8.89 us -> none  [the longest x1 4.44 us: expert_apply(): up_part = jnp.dot(flat_rows, up_local, preferred_element_type=jnp.float32)]
    reduce_sum x3 -> x0, other arithmetic: 6.35 us -> none  [the longest x1 6.24 us: shards(): jnp.sum(gate_norm[:, :, None] * picked.astype(jnp.float32), axis=1)]
    all_to_all x1 -> x0, starting transfers between devices: 5.88 us -> none  [shards(): lax.all_to_all(results, 'expert', split_axis=0, concat_axis=0, tiled=True)]
  transfers between devices with their start and end apart: 3 -> 0, of which waited for: 3 -> 0; matrix products, arithmetic and copies ran while one was open for 3% -> 0% of each run, Pallas kernels for 0% -> 0%
where the time goes in v2:
time: 101 us
  Pallas kernels  99.1 us (98%)
  local copies, waits for them, and re-layouts  1.88 us (2%)
    pallas_call x1, Pallas kernels, shards(): pl.pallas_call(functools.partial(layer_kernel, n, chunks, ring), out_shap...  99.1 us

profile of v2, /device:TPU:0, one launch (start us, length us, event | category | flops | bytes accessed | tf_op | source)
XLA Modules:
  0.0 100.9 jit_solution(13389887147356996399)
XLA Ops:
  0.0 99.1 %shard_map.64 = bf16[128,2048]{1,0:T(8,128)(2,1)} custom-call(s32[2,128]{1,0:T(2,128)} %bitcast.2, f32[2,128]{1,0:T(2,128)} %bitcast.3, bf16[128,2048]{1,0:T(8,128)(2,1)} %tok_ref.1, bf16[1,2048,768]{2,1,0:T(8,128)(2,1)} %wg_hbm.1, bf16[1,2048,768]{2,1,0:T(8,128)(2,1)} %wu_hbm.1, bf16[1,768,2048]{2,1,0:T(8,128)(2,1)} %wd_hbm.1), custom_call_target="tpu_custom_call" | custom-call | tf_op jit(solution)/shard_map/pallas_call | solution.py:258
  99.1 1.9 %copy.8 = bf16[128,2048]{1,0:T(8,128)(2,1)} copy(bf16[128,2048]{1,0:T(8,128)(2,1)} %shard_map.64) | data formatting | bytes 1048576
